TPU v7x, 512 devices: a whole 4x8x8 slice. The times are simulated.
512 devices in a mesh: group: 16 (over z, core), dom: 32 (over y, x).
Axes of the slice: x: 4, y: 8, z: 8, core: 2. Of those that a mesh axis runs over, the one named last changes fastest.
Arguments:
- state: float32 [5, 393216], P(None, ('group', 'dom')), may hold values from -0.5 to 1.6, as said below
- pinv: bfloat16 [20, 40, 393216], P(None, None, ('group', 'dom')), may hold values from -0.21875 to 0.21875
- stencil: int32 [40, 393216], P(None, ('group', 'dom')), may hold values from 0 to 3071, as said below
- send_ids: int32 [16384, 64], P(('group', 'dom')), may hold values from 0 to 767
- group_ids: int32 [1024, 128], P(('group', 'dom')), may hold values from 0 to 767
- face_cells: int32 [2, 786432], P(None, ('group', 'dom')), may hold values from 0 to 3007, as said below
- face_geom: float32 [4, 786432], P(None, ('group', 'dom')), may hold values from -1 to 1, as said below
- face_basis: bfloat16 [80, 786432], P(None, ('group', 'dom')), may hold values from -3 to 3
Outputs:
- residual: float32 [5, 393216], P(None, ('group', 'dom'))
Inputs may be any that keep to these rules, and one draw needn't show every extreme that they name: `stencil`: for a cell of partition g * 32 + d every entry is an own cell, or a column 768 + p * 64 + q where p differs from d in exactly one bit, or a column of the lower group block only if g > 0, of the upper only if g < 15. `face_cells`: row 0 is an own cell; row 1 is another own cell or a column that a stencil of the same partition may read, within the first 32 slots of a block of the same group or the first 64 slots of a group block. `face_geom`: rows 0 to 2 form a unit normal; row 3 is the area, from 0.2 to 1. `state`: density and pressure from 0.6 to 1.6, velocity components from -0.5 to 0.5.
All inputs are finite; a program needn't handle non-finite values.
Results may differ from a plain program's by a relative error of at most 0.0022.
Values sent between devices are 32-bit elements; how exact they have to be, the bound alone decides.
A program may use at most 64 MiB of HBM per device.

v0:
```python
import jax
import jax.numpy as jnp
from jax import lax
from jax.sharding import PartitionSpec as P

GAMMA = 1.4
FLOOR = 0.2


def passed_along(block, axis, distance):
    devices = range(lax.axis_size(axis))
    route = [(i - distance, i) for i in devices if i - distance in devices]
    return lax.ppermute(block, axis, route)


def physical_flux(rho, velocity, pressure, normal):
    normal_speed = jnp.sum(velocity * normal, axis=0)
    energy = (
        GAMMA / (GAMMA - 1.0) * pressure + 0.5 * rho * jnp.sum(velocity * velocity, axis=0)
    ) * normal_speed
    momentum = rho * velocity * normal_speed + pressure * normal
    return jnp.concatenate([(rho * normal_speed)[None], momentum, energy[None]], axis=0)


def entropy_fixed(eigen, sound):
    delta = 0.1 * sound
    magnitude = jnp.abs(eigen)
    return jnp.where(magnitude < delta, (eigen * eigen + delta * delta) / (2.0 * delta), magnitude)


def roe_flux(left, right, normal):
    rho_left, vel_left, pres_left = (left[0], left[1:4], left[4])
    rho_right, vel_right, pres_right = (right[0], right[1:4], right[4])
    root_left = jnp.sqrt(rho_left)
    root_right = jnp.sqrt(rho_right)
    weights = root_left + root_right
    rho_avg = root_left * root_right
    vel_avg = (root_left * vel_left + root_right * vel_right) / weights
    enth_left = GAMMA / (GAMMA - 1.0) * pres_left / rho_left + 0.5 * jnp.sum(
        vel_left * vel_left, axis=0
    )
    enth_right = GAMMA / (GAMMA - 1.0) * pres_right / rho_right + 0.5 * jnp.sum(
        vel_right * vel_right, axis=0
    )
    enth_avg = (root_left * enth_left + root_right * enth_right) / weights
    speed_sq = jnp.sum(vel_avg * vel_avg, axis=0)
    sound_sq = (GAMMA - 1.0) * (enth_avg - 0.5 * speed_sq)
    sound = jnp.sqrt(sound_sq)
    normal_avg = jnp.sum(vel_avg * normal, axis=0)
    d_rho = rho_right - rho_left
    d_pres = pres_right - pres_left
    d_vel = vel_right - vel_left
    d_normal = jnp.sum(d_vel * normal, axis=0)
    wave_one = (
        entropy_fixed(normal_avg - sound, sound)
        * (d_pres - rho_avg * sound * d_normal)
        / (2.0 * sound_sq)
    )
    wave_five = (
        entropy_fixed(normal_avg + sound, sound)
        * (d_pres + rho_avg * sound * d_normal)
        / (2.0 * sound_sq)
    )
    middle = entropy_fixed(normal_avg, sound)
    wave_two = middle * (d_rho - d_pres / sound_sq)
    ones = jnp.ones_like(rho_avg)
    first = jnp.concatenate(
        [ones[None], vel_avg - sound * normal, (enth_avg - sound * normal_avg)[None]], axis=0
    )
    second = jnp.concatenate([ones[None], vel_avg, (0.5 * speed_sq)[None]], axis=0)
    shear = jnp.concatenate(
        [
            jnp.zeros_like(rho_avg)[None],
            d_vel - d_normal * normal,
            (jnp.sum(vel_avg * d_vel, axis=0) - normal_avg * d_normal)[None],
        ],
        axis=0,
    )
    fifth = jnp.concatenate(
        [ones[None], vel_avg + sound * normal, (enth_avg + sound * normal_avg)[None]], axis=0
    )
    dissipation = (
        wave_one * first + wave_two * second + middle * rho_avg * shear + wave_five * fifth
    )
    total = physical_flux(rho_left, vel_left, pres_left, normal) + physical_flux(
        rho_right, vel_right, pres_right, normal
    )
    return 0.5 * total - 0.5 * dissipation


def floored(values):
    return jnp.concatenate(
        [jnp.maximum(values[0:1], FLOOR), values[1:4], jnp.maximum(values[4:5], FLOOR)], axis=0
    )


def face_residual(value_table, coef_table, face_cells, face_geom, face_basis, count):
    faces = face_cells.shape[1]
    basis = face_basis.astype(jnp.float32).reshape(2, 2, 20, faces)
    normal = face_geom[0:3]
    area = face_geom[3]
    packed = jnp.concatenate([value_table, coef_table], axis=0).T
    sides = []
    for side in range(2):
        gathered = jnp.take(packed, face_cells[side], axis=0).T
        centre = gathered[0:5]
        terms = gathered[5:].reshape(5, 20, faces)
        points = []
        for point in range(2):
            points.append(floored(centre + jnp.sum(terms * basis[side, point][None], axis=1)))
        sides.append(points)
    flux = roe_flux(sides[0][0], sides[1][0], normal) + roe_flux(sides[0][1], sides[1][1], normal)
    weighted = 0.5 * area * flux
    columns = jnp.arange(count, dtype=jnp.int32)[None, :]
    incidence = (face_cells[0][:, None] == columns).astype(jnp.float32) - (
        face_cells[1][:, None] == columns
    ).astype(jnp.float32)
    return jnp.dot(
        weighted, incidence, precision=lax.Precision.HIGHEST, preferred_element_type=jnp.float32
    )


def layer_blocks(rows, group_ids, width, mover):
    upward = jnp.take(rows, group_ids[0, :width], axis=1)
    downward = jnp.take(rows, group_ids[1, :width], axis=1)
    return (mover(upward, 1), mover(downward, -1))


def per_device(state, pinv, stencil, send_ids, group_ids, face_cells, face_geom, face_basis):
    cells = state.shape[1]
    layer_size = group_ids.shape[1]
    sten_count = stencil.shape[0]
    picked = jnp.take(state, send_ids.reshape(-1), axis=1)
    beside = lax.all_to_all(picked, "dom", split_axis=1, concat_axis=1, tiled=True)
    lower, upper = layer_blocks(
        state, group_ids, layer_size, lambda block, offset: passed_along(block, "group", offset)
    )
    value_table = jnp.concatenate([state, beside, lower, upper], axis=1)
    value_rows = value_table.T
    near = (
        jnp.take(value_rows, stencil.reshape(-1), axis=0)
        .reshape(sten_count, cells, 5)
        .transpose(2, 0, 1)
    )
    diffs = (near - state[:, None, :]).astype(jnp.bfloat16)
    coefs = jnp.einsum("kjc,vjc->vkc", pinv, diffs, preferred_element_type=jnp.float32).reshape(
        100, cells
    )
    chosen_ids = send_ids.reshape(-1)
    coef_picked = jnp.take(coefs, chosen_ids, axis=1)
    coef_beside = lax.all_to_all(coef_picked, "dom", split_axis=1, concat_axis=1, tiled=True)
    coef_lower, coef_upper = layer_blocks(
        coefs, group_ids, layer_size, lambda block, offset: passed_along(block, "group", offset)
    )
    coef_table = jnp.concatenate([coefs, coef_beside, coef_lower, coef_upper], axis=1)
    return face_residual(value_table, coef_table, face_cells, face_geom, face_basis, cells)


def solution(mesh):
    in_specs = (
        P(None, ("group", "dom")),
        P(None, None, ("group", "dom")),
        P(None, ("group", "dom")),
        P(("group", "dom"), None),
        P(("group", "dom"), None),
        P(None, ("group", "dom")),
        P(None, ("group", "dom")),
        P(None, ("group", "dom")),
    )
    out_specs = P(None, ("group", "dom"))
    return jax.shard_map(
        per_device, mesh=mesh, in_specs=in_specs, out_specs=out_specs, check_vma=False
    )
```

profile of v0, /device:TPU:195, one launch (start us, length us, event | category | flops | bytes accessed | tf_op | source)
XLA Modules:
  0.0 221.9 jit_solution(16691789823853166769)
XLA Ops:
  0.0 0.9 copy.382
  2.5 5.8 %collective-permute-start = (f32[5,128]{0,1:T(8,128)S(1)}, f32[5,128]{0,1:T(8,128)S(1)}, u32[]{:S(2)}, u32[]{:S(2)}) collective-permute-start(f32[5,128]{0,1:T(8,128)S(1)} %select_bitcast_fusion.5), channel_id=1, source_target_pairs={{0,32},{32,64},{64,96},{96,128},{128,160},{160,192},{192,224},{224... | collective-permute-start | bytes 7688 | tf_op jit(solution)/shard_map/ppermute | solution.py:13
  9.1 1.9 collective-permute-start.1
  11.0 0.8 reshape.310
  12.6 5.5 %gather_fusion = f32[2048,5]{1,0:T(8,128)S(1)} fusion(f32[5,768]{0,1:T(8,128)S(1)} %copy.382, s32[2048]{0:T(1024)S(1)} %broadcast_clamp_fusion.1), kind=kCustom, calls=%fused_computation.6 | custom fusion | bytes 90112 | tf_op jit(solution)/shard_map/jit(_take)/gather | solution.py:133
  19.2 9.7 %all-to-all-start = ((f32[32,1,320]{2,1,0:T(1,128)}), f32[32,1,320]{2,1,0:T(1,128)S(1)}, u32[]{:S(2)}, u32[]{:S(2)}) async-start(f32[32,1,320]{2,1,0:T(1,128)} %reshape.439), calls=%async_computation | async-start | bytes 98304 | tf_op jit(solution)/shard_map/all_to_all | solution.py:134
  29.9 4.3 %copy.387 = bf16[20,40,768]{1,0,2:T(8,128)(2,1)} copy(bf16[20,40,768]{2,1,0:T(8,128)(2,1)S(1)} %copy-done.4) | data formatting | bytes 2457600 | tf_op args[1]
  34.2 0.8 copy.384
  35.1 1.6 all-to-all-done
  39.5 101.4 %gather_fusion.1 = f32[30720,5]{1,0:T(8,128)} fusion(f32[3072,5]{1,0:T(8,128)S(1)} %maximum_bitcast_fusion, s32[30720]{0:T(1024)S(1)} %broadcast_clamp_fusion), kind=kCustom, calls=%fused_computation.7 | custom fusion | bytes 1351680 | tf_op jit(solution)/shard_map/jit(_take)/gather | solution.py:141
  140.9 10.8 %copy.385 = f32[40,768,5]{0,2,1:T(8,128)S(1)} copy(f32[40,768,5]{2,1,0:T(8,128)} %bitcast.60) | data formatting | bytes 1228800 | tf_op jit(solution)/shard_map/jit(_take)/gather | solution.py:141
  151.7 6.7 %convolution_bitcast_fusion = f32[5,20,768]{1,0,2:T(8,128)} fusion(bf16[20,40,768]{1,0,2:T(8,128)(2,1)} %copy.387, f32[40,768,5]{0,2,1:T(8,128)S(1)} %copy.385, f32[5,768]{0,1:T(8,128)S(1)} %copy.382, pred[40,768]{0,1:T(8,128)(4,1)} %copy.384), kind=kOutput, calls=%fused_computation.19 | convolution fusion | flops 6604800 | bytes 2196480 | tf_op jit(solution)/shard_map/kjc,vjc->vkc/dot_general | solution.py:146
  158.4 2.1 reshape.409
  160.6 5.5 %gather_fusion.2 = f32[2048,100]{1,0:T(8,128)S(1)} fusion(f32[100,768]{0,1:T(8,128)S(1)} %reshape.409, s32[2048]{0:T(1024)S(1)} %broadcast_clamp_fusion.1), kind=kCustom, calls=%fused_computation.8 | custom fusion | bytes 1646592 | tf_op jit(solution)/shard_map/jit(_take)/gather | solution.py:150
  166.0 1.3 broadcast_select_fusion
  167.4 7.7 %all-to-all-start.1 = ((f32[100,32,64]{0,2,1:T(8,128)}), f32[100,32,64]{0,2,1:T(8,128)S(1)}, u32[]{:S(2)}, u32[]{:S(2)}) async-start(f32[100,32,64]{0,2,1:T(8,128)} %broadcast_select_fusion), calls=%async_computation.1 | async-start | bytes 2097152 | tf_op jit(solution)/shard_map/all_to_all | solution.py:151
  175.7 1.1 reshape.318
  176.8 1.3 pad_clamp_fusion
  178.1 1.4 multiply_reduce_fusion.24
  180.1 0.9 slice_bitcast_fusion.2
  183.1 6.0 %collective-permute-start.2 = (f32[100,128]{0,1:T(8,128)S(1)}, f32[100,128]{0,1:T(8,128)S(1)}, u32[]{:S(2)}, u32[]{:S(2)}) collective-permute-start(f32[100,128]{0,1:T(8,128)S(1)} %select_bitcast_fusion.3), channel_id=1, source_target_pairs={{0,32},{32,64},{64,96},{96,128},{128,160},{160,192},{192,224},{224... | collective-permute-start | bytes 153608 | tf_op jit(solution)/shard_map/ppermute | solution.py:13
  189.8 2.1 collective-permute-start.3
  191.9 1.3 pad_clamp_fusion.1
  194.3 2.6 %collective-permute-done.3 = f32[100,128]{0,1:T(8,128)S(1)} collective-permute-done((f32[100,128]{0,1:T(8,128)S(1)}, f32[100,128]{0,1:T(8,128)S(1)}, u32[]{:S(2)}, u32[]{:S(2)}) %collective-permute-start.3) | collective-permute-done | bytes 51232 | tf_op jit(solution)/shard_map/ppermute | solution.py:13
  196.9 6.3 %all-to-all-done.1 = f32[100,32,64]{0,2,1:T(8,128)S(1)} async-done(((f32[100,32,64]{0,2,1:T(8,128)}), f32[100,32,64]{0,2,1:T(8,128)S(1)}, u32[]{:S(2)}, u32[]{:S(2)}) %all-to-all-start.1) | async-done | bytes 819232 | tf_op jit(solution)/shard_map/all_to_all | solution.py:151
  203.2 1.0 copy-done.2
  204.2 1.7 maximum_bitcast_fusion.1
  205.9 3.0 %gather_fusion.8 = f32[1536,105]{1,0:T(8,128)S(1)} fusion(f32[3072,105]{1,0:T(8,128)S(1)} %maximum_bitcast_fusion.1, s32[2048]{0:T(1024)} %pad_clamp_fusion), kind=kCustom, calls=%fused_computation.5.clone | custom fusion | bytes 1296384 | tf_op jit(solution)/shard_map/jit(_take)/gather | solution.py:105
  209.3 0.8 copy-done.3
  210.9 2.6 %gather_fusion.7 = f32[1536,105]{1,0:T(8,128)S(1)} fusion(f32[3072,105]{1,0:T(8,128)S(1)} %maximum_bitcast_fusion.1, s32[2048]{0:T(1024)S(1)} %copy-done.18), kind=kCustom, calls=%fused_computation.2.clone | custom fusion | bytes 1296384 | tf_op jit(solution)/shard_map/jit(_take)/gather | solution.py:105
  215.1 0.8 slice_add_fusion
  217.6 4.3 %fusion = f32[5,768]{1,0:T(8,128)} fusion(s32[1536]{0:T(1024)S(1)} %copy-done.14, s32[1536]{0:T(1024)S(1)} %get-tuple-element.50, f32[1,1536]{1,0:T(1,128)S(1)} %get-tuple-element.88, f32[3,1536]{1,0:T(4,128)S(1)} %get-tuple-element.92, f32[1,1536]{1,0:T(1,128)S(1)} %get-tuple-element.89, f32[1,1536]{1,0:T(1,128)S(1)} %get-tuple-element.90, ...), kind=kOutput, calls=%fused_computation.9 | convolution fusion | flops 77045760 | bytes 402472 | tf_op jit(solution)/shard_map/dot_general | solution.py:118
  (114 shorter events, 17.2 us)
Async XLA Ops:
  0.0 28.9 %copy-start.9 = (s32[40,768]{1,0:T(8,128)S(1)}, s32[40,768]{1,0:T(8,128)}, u32[]{:S(2)}) copy-start(s32[40,768]{1,0:T(8,128)} %param.16) | copy-start | bytes 368644
  1.7 7.2 %copy-start.25 = (pred[128]{0:T(512)(128)(4,1)}, pred[128]{0:T(512)(128)(4,1)S(1)}, u32[]{:S(2)}) copy-start(pred[128]{0:T(512)(128)(4,1)S(1)} %get-tuple-element.110) | copy-start | bytes 388
  1.7 7.2 %copy-start.26 = (pred[128]{0:T(512)(128)(4,1)}, pred[128]{0:T(512)(128)(4,1)S(1)}, u32[]{:S(2)}) copy-start(pred[128]{0:T(512)(128)(4,1)S(1)} %get-tuple-element.62) | copy-start | bytes 388
  1.8 10.8 %copy-start.23 = (s32[1024]{0:T(1024)}, s32[1024]{0:T(1024)S(1)}, u32[]{:S(2)}) copy-start(s32[1024]{0:T(1024)S(1)} %pad_clamp_fusion.3) | copy-start | bytes 12292
  2.5 36.0 %collective-permute-start = (f32[5,128]{0,1:T(8,128)S(1)}, f32[5,128]{0,1:T(8,128)S(1)}, u32[]{:S(2)}, u32[]{:S(2)}) collective-permute-start(f32[5,128]{0,1:T(8,128)S(1)} %select_bitcast_fusion.5), channel_id=1, source_target_pairs={{0,32},{32,64},{64,96},{96,128},{128,160},{160,192},{192,224},{224... | collective-permute-start | bytes 7688 | tf_op jit(solution)/shard_map/ppermute | solution.py:13
  8.3 4.3 %copy-start.24 = (s32[1024]{0:T(1024)}, s32[1024]{0:T(1024)S(1)}, u32[]{:S(2)}) copy-start(s32[1024]{0:T(1024)S(1)} %pad_clamp_fusion.2) | copy-start | bytes 12292
  9.1 29.5 %collective-permute-start.1 = (f32[5,128]{0,1:T(8,128)S(1)}, f32[5,128]{0,1:T(8,128)S(1)}, u32[]{:S(2)}, u32[]{:S(2)}) collective-permute-start(f32[5,128]{0,1:T(8,128)S(1)} %select_bitcast_fusion.4), channel_id=1, source_target_pairs={{32,0},{64,32},{96,64},{128,96},{160,128},{192,160},{224,192},{256... | collective-permute-start | bytes 7688 | tf_op jit(solution)/shard_map/ppermute | solution.py:13
  12.5 16.8 %copy-start.16 = (pred[32,64]{1,0:T(8,128)(4,1)}, pred[32,64]{1,0:T(8,128)(4,1)S(1)}, u32[]{:S(2)}) copy-start(pred[32,64]{1,0:T(8,128)(4,1)S(1)} %compare_and_fusion.1) | copy-start | bytes 6148
  12.6 16.7 %copy-start.19 = (s32[2,1536]{1,0:T(2,128)S(1)}, s32[2,1536]{1,0:T(2,128)}, u32[]{:S(2)}) copy-start(s32[2,1536]{1,0:T(2,128)} %param.19) | copy-start | bytes 36868
  12.6 17.3 %copy-start.4 = (bf16[20,40,768]{2,1,0:T(8,128)(2,1)S(1)}, bf16[20,40,768]{2,1,0:T(8,128)(2,1)}, u32[]{:S(2)}) copy-start(bf16[20,40,768]{2,1,0:T(8,128)(2,1)} %param.15) | copy-start | bytes 3686404
  19.2 17.5 %all-to-all-start = ((f32[32,1,320]{2,1,0:T(1,128)}), f32[32,1,320]{2,1,0:T(1,128)S(1)}, u32[]{:S(2)}, u32[]{:S(2)}) async-start(f32[32,1,320]{2,1,0:T(1,128)} %reshape.439), calls=%async_computation | async-start | bytes 98304 | tf_op jit(solution)/shard_map/all_to_all | solution.py:134
  38.5 1.0 copy-start
  38.5 1.0 copy-start.10
  38.5 1.0 copy-start.12
  160.5 5.5 %copy-start.17 = (pred[32,64]{1,0:T(8,128)(4,1)S(1)}, pred[32,64]{1,0:T(8,128)(4,1)}, u32[]{:S(2)}) copy-start(pred[32,64]{1,0:T(8,128)(4,1)} %copy-done.16) | copy-start | bytes 6148
  167.4 7.7 %copy-start.14 = (s32[1536]{0:T(1024)S(1)}, s32[1536]{0:T(1024)}, u32[]{:S(2)}) copy-start(s32[1536]{0:T(1024)} %get-tuple-element.51) | copy-start | bytes 18436
  167.4 35.8 %all-to-all-start.1 = ((f32[100,32,64]{0,2,1:T(8,128)}), f32[100,32,64]{0,2,1:T(8,128)S(1)}, u32[]{:S(2)}, u32[]{:S(2)}) async-start(f32[100,32,64]{0,2,1:T(8,128)} %broadcast_select_fusion), calls=%async_computation.1 | async-start | bytes 2097152 | tf_op jit(solution)/shard_map/all_to_all | solution.py:151
  175.7 28.5 %copy-start.1 = (f32[5,32,64]{0,2,1:T(8,128)S(1)}, f32[5,32,64]{0,2,1:T(8,128)}, u32[]{:S(2)}) copy-start(f32[5,32,64]{0,2,1:T(8,128)} %copy-done) | copy-start | bytes 122884
  175.7 28.5 %copy-start.11 = (f32[5,128]{0,1:T(8,128)S(1)}, f32[5,128]{0,1:T(8,128)}, u32[]{:S(2)}) copy-start(f32[5,128]{0,1:T(8,128)} %copy-done.10) | copy-start | bytes 7684
  183.1 11.2 %collective-permute-start.2 = (f32[100,128]{0,1:T(8,128)S(1)}, f32[100,128]{0,1:T(8,128)S(1)}, u32[]{:S(2)}, u32[]{:S(2)}) collective-permute-start(f32[100,128]{0,1:T(8,128)S(1)} %select_bitcast_fusion.3), channel_id=1, source_target_pairs={{0,32},{32,64},{64,96},{96,128},{128,160},{160,192},{192,224},{224... | collective-permute-start | bytes 153608 | tf_op jit(solution)/shard_map/ppermute | solution.py:13
  189.8 7.1 %collective-permute-start.3 = (f32[100,128]{0,1:T(8,128)S(1)}, f32[100,128]{0,1:T(8,128)S(1)}, u32[]{:S(2)}, u32[]{:S(2)}) collective-permute-start(f32[100,128]{0,1:T(8,128)S(1)} %select_bitcast_fusion.2), channel_id=1, source_target_pairs={{32,0},{64,32},{96,64},{128,96},{160,128},{192,160},{224,192},{256... | collective-permute-start | bytes 153608 | tf_op jit(solution)/shard_map/ppermute | solution.py:13
  196.9 6.3 %copy-start.15 = (f32[100,128]{0,1:T(8,128)}, f32[100,128]{0,1:T(8,128)S(1)}, u32[]{:S(2)}) copy-start(f32[100,128]{0,1:T(8,128)S(1)} %collective-permute-done.3) | copy-start | bytes 153604
  203.2 1.0 copy-start.2
  205.9 3.3 %copy-start.21 = (pred[1536]{0:T(1024)(128)(4,1)S(1)}, pred[1536]{0:T(1024)(128)(4,1)}, u32[]{:S(2)}) copy-start(pred[1536]{0:T(1024)(128)(4,1)} %get-tuple-element.114) | copy-start | bytes 4612
  210.9 2.9 %copy-start.20 = (pred[1536]{0:T(1024)(128)(4,1)S(1)}, pred[1536]{0:T(1024)(128)(4,1)}, u32[]{:S(2)}) copy-start(pred[1536]{0:T(1024)(128)(4,1)} %get-tuple-element.115) | copy-start | bytes 4612
  213.9 1.0 copy-start.8
  213.9 2.0 copy-start.5
  214.0 2.0 copy-start.6
  214.0 2.5 %copy-start.13 = (f32[4,1536]{1,0:T(4,128)S(1)}, f32[4,1536]{1,0:T(4,128)}, u32[]{:S(2)}) copy-start(f32[4,1536]{1,0:T(4,128)} %param.20) | copy-start | bytes 73732
  215.9 1.7 copy-start.22
  215.9 1.7 copy-start.27
  215.9 1.7 copy-start.28
  (3 other events, 2.5 us)
where the time goes:
time: 223 us; the launch traced here: 222 us
  local copies, waits for them, and re-layouts  152 us (68%)
  starting transfers between devices  33.2 us (15%)
  other arithmetic  15 us (7%)
  matrix products  10.9 us (5%)
  waiting for transfers between devices  10.5 us (5%)
    gather x2, local copies, waits for them, and re-layouts, per_device(): jnp.take(value_rows, stencil.reshape(-1), axis=0)  112 us
    ppermute x4, starting transfers between devices, passed_along(): return lax.ppermute(block, axis, route)  15.8 us
    unnamed x63, local copies, waits for them, and re-layouts  10.3 us
    all_to_all x1, starting transfers between devices, per_device(): lax.all_to_all(picked, 'dom', split_axis=1, concat_axis=1, tiled=True)  9.69 us
    all_to_all x1, starting transfers between devices, per_device(): lax.all_to_all(coef_picked, 'dom', split_axis=1, concat_axis=1, tiled=True)  7.72 us
    dot_general x1, matrix products, per_device(): jnp.einsum('kjc,vjc->vkc', pinv, diffs, preferred_element_type=jnp.float32)  6.68 us
    all_to_all x1, waiting for transfers between devices, per_device(): lax.all_to_all(coef_picked, 'dom', split_axis=1, concat_axis=1, tiled=True)  6.3 us
    gather x4, local copies, waits for them, and re-layouts, face_residual(): gathered = jnp.take(packed, face_cells[side], axis=0).T  6.19 us
  transfers between devices with their start and end apart: 6, of which 3 were waited for; matrix products, arithmetic and copies ran while one was open for 13% of the time, Pallas kernels for 0%

commit v1 on v0

v1 whole, which is shorter than its diff:
```python
import functools

import jax
import jax.numpy as jnp
from jax import lax
from jax.experimental import pallas as pl
from jax.experimental.pallas import tpu as pltpu
from jax.sharding import PartitionSpec as P

GAMMA = 1.4
FLOOR = 0.2
MESH = pl.DeviceIdType.MESH
F32 = jnp.float32
BF16 = jnp.bfloat16
I32 = jnp.int32

CELLS = 768
FACES = 1536
CT = CELLS // 128
FT = FACES // 128
COEF = 20
STEN = 40
JT = STEN // 8
ROWS = 13
BITS = 5
UT = FT // 4


def loop(count, body):
    def step(i, carry):
        body(i)
        return carry

    lax.fori_loop(0, count, step, 0)


def lanes_at(tile):
    return pl.ds(pl.multiple_of(tile * 128, 128), 128)


def lane_gather(values, lanes):
    return jnp.take_along_axis(values, lanes, axis=1, mode="promise_in_bounds")


def wide(row):
    return jnp.broadcast_to(row, (8, 128))


def iota(axis):
    return lax.broadcasted_iota(I32, (8, 128), axis)


def merged(first, second, distance):
    mask = (iota(0) & distance) == 0
    kept = jnp.where(mask, first, second)
    moved = jnp.where(mask, second, first)
    return kept + pltpu.roll(moved, distance, 0)


def row_sums(parts):
    for distance in (1, 2, 4):
        parts = [merged(parts[i], parts[i + 1], distance) for i in range(0, len(parts), 2)]
    return parts[0]


def selected(tiles, lanes, tile, start, acc):
    for i, values in enumerate(tiles):
        got = lane_gather(values, lanes)
        acc = got if acc is None else jnp.where(tile == start + i, got, acc)
    return acc


def table_index(slot, column):
    flip = lax.shift_right_arithmetic(slot - 768, 6) ^ column
    bit = (flip >> 1) - (flip >> 3) - 2 * (flip >> 4)
    near = 768 + bit * 64 + (slot & 63)
    return jnp.where(slot < 768, slot, jnp.where(slot < 2816, near, slot - 1664))


def coef_index(slot, column):
    flip = lax.shift_right_arithmetic(slot - 768, 6) ^ column
    bit = (flip >> 1) - (flip >> 3) - 2 * (flip >> 4)
    near = jnp.where(bit < 4, 768 + bit * 32, 1024) + (slot & 31)
    far = 896 + jnp.where(slot < 2944, 0, 64) + (slot & 63)
    return jnp.where(slot < 768, slot, jnp.where(slot < 2816, near, far))


def physical(w, n, vn):
    rho, u, v, q, p = w
    kinetic = 0.5 * rho * (u * u + v * v + q * q)
    mass = rho * vn
    energy = (GAMMA / (GAMMA - 1.0) * p + kinetic) * vn
    return mass, mass * u + p * n[0], mass * v + p * n[1], mass * q + p * n[2], energy, kinetic


def entropy_fixed(eigen, sound):
    delta = 0.1 * sound
    magnitude = jnp.abs(eigen)
    return jnp.where(magnitude < delta, (eigen * eigen + delta * delta) / (2.0 * delta), magnitude)


def dot3(a, b):
    return a[0] * b[0] + a[1] * b[1] + a[2] * b[2]


def roe_flux(left, right, n):
    rho_l, u_l, p_l = left[0], left[1:4], left[4]
    rho_r, u_r, p_r = right[0], right[1:4], right[4]
    vn_l, vn_r = dot3(u_l, n), dot3(u_r, n)
    flux_l = physical(left, n, vn_l)
    flux_r = physical(right, n, vn_r)
    root_l, root_r = jnp.sqrt(rho_l), jnp.sqrt(rho_r)
    inverse = 1.0 / (root_l + root_r)
    part_l, part_r = root_l * inverse, root_r * inverse
    rho_a = root_l * root_r
    ratio = GAMMA / (GAMMA - 1.0)
    enth_l = (ratio * p_l + flux_l[5]) / rho_l
    enth_r = (ratio * p_r + flux_r[5]) / rho_r
    u_a = [part_l * a + part_r * b for a, b in zip(u_l, u_r)]
    enth_a = part_l * enth_l + part_r * enth_r
    half_speed = 0.5 * dot3(u_a, u_a)
    sound_sq = (GAMMA - 1.0) * (enth_a - half_speed)
    sound = jnp.sqrt(sound_sq)
    vn_a = dot3(u_a, n)
    d_rho, d_p = rho_r - rho_l, p_r - p_l
    d_u = [b - a for a, b in zip(u_l, u_r)]
    d_vn = dot3(d_u, n)
    per_sq = 1.0 / sound_sq
    slope = rho_a * sound * d_vn
    wave_1 = entropy_fixed(vn_a - sound, sound) * (d_p - slope) * (0.5 * per_sq)
    wave_5 = entropy_fixed(vn_a + sound, sound) * (d_p + slope) * (0.5 * per_sq)
    middle = entropy_fixed(vn_a, sound)
    wave_2 = middle * (d_rho - d_p * per_sq)
    shear = middle * rho_a
    both = wave_1 + wave_5
    total = both + wave_2
    across = sound * (wave_5 - wave_1)
    out = [flux_l[0] + flux_r[0] - total]
    tilt = across - shear * d_vn
    for i in range(3):
        out.append(flux_l[1 + i] + flux_r[1 + i] - (total * u_a[i] + tilt * n[i] + shear * d_u[i]))
    energy = (
        both * enth_a
        + across * vn_a
        + wave_2 * half_speed
        + shear * (dot3(u_a, d_u) - vn_a * d_vn)
    )
    out.append(flux_l[4] + flux_r[4] - energy)
    return out


def floored(w):
    return [jnp.maximum(w[0], FLOOR), w[1], w[2], w[3], jnp.maximum(w[4], FLOOR)]


def polynomials(coefs, side, tile, basis, part):
    low = iota(0) < 4
    place = (tile // 4) * 8 + tile % 4
    for point in range(2):
        terms = [coefs[r] * basis[side * 2 + point, r % 5, tile] for r in range(ROWS)]
        split = {r: (jnp.where(low, terms[r], 0.0), jnp.where(low, 0.0, terms[r])) for r in (2, 7)}
        sums = [
            terms[0] + terms[1] + split[2][0],
            split[2][1] + terms[3] + terms[4],
            terms[5] + terms[6] + split[7][0],
            split[7][1] + terms[8] + terms[9],
            terms[10] + terms[11] + jnp.where(low, terms[12], 0.0),
        ]
        for v in range(5):
            part[v, place + 4 * point] = sums[v]


def kernel(
    groups,
    state_h, pinv_h, sten_h, send_h, gids_h, fc_h, fg_h, fb_h,
    out_ref,
    st, pb, sn, sd, gi, fc, fg, fb,
    tbl, snd1, rcv1, snd2, rcv2, snd3, rcv3,
    nidx, pf, near, ctab, rgat, gtab, bas, bf32, inc, slots, geo,
    part, cen, left_w, wrow, wl,
    in_sem, s1, r1, s2, r2,
):
    g = lax.axis_index("group")
    d = lax.axis_index("dom")
    beside = [d + (1 << b) * (1 - 2 * ((d // (1 << b)) % 2)) for b in range(BITS)]
    has_low = g > 0
    has_high = g < groups - 1

    pairs = [(state_h, st), (send_h, sd), (gids_h, gi), (sten_h, sn), (pinv_h, pb), (fc_h, fc), (fb_h, fb), (fg_h, fg)]
    loads = [pltpu.make_async_copy(a, b, in_sem.at[i]) for i, (a, b) in enumerate(pairs)]
    for load in loads:
        load.start()

    barrier = pltpu.get_barrier_semaphore()
    for b in range(BITS):
        pl.semaphore_signal(barrier, inc=1, device_id=(g, beside[b]), device_id_type=MESH)

    @pl.when(has_low)
    def _():
        pl.semaphore_signal(barrier, inc=1, device_id=(g - 1, d), device_id_type=MESH)

    @pl.when(has_high)
    def _():
        pl.semaphore_signal(barrier, inc=1, device_id=(g + 1, d), device_id_type=MESH)

    def exchange(near_src, near_dst, far_src, far_dst, send, recv):
        copies = [
            pltpu.make_async_remote_copy(
                src_ref=near_src.at[b],
                dst_ref=near_dst.at[b],
                send_sem=send.at[b],
                recv_sem=recv.at[b],
                device_id=(g, beside[b]),
                device_id_type=MESH,
            )
            for b in range(BITS)
        ]
        up, down = [
            pltpu.make_async_remote_copy(
                src_ref=far_src(i),
                dst_ref=far_dst(i),
                send_sem=send.at[BITS + i],
                recv_sem=recv.at[BITS + i],
                device_id=(g + 1 - 2 * i, d),
                device_id_type=MESH,
            )
            for i in range(2)
        ]
        return copies, up, down

    def start(copies, up, down):
        for b in reversed(range(BITS)):
            copies[b].start()
        pl.when(has_high)(up.start)
        pl.when(has_low)(down.start)

    def received(copies, up, down):
        for copy in copies:
            copy.wait_recv()
        pl.when(has_low)(up.wait_recv)
        pl.when(has_high)(down.wait_recv)

    def sent(copies, up, down):
        for copy in copies:
            copy.wait_send()
        pl.when(has_high)(up.wait_send)
        pl.when(has_low)(down.wait_send)

    lane = iota(1)
    lower_half = lane < 64
    quarter = lane >> 5

    for load in loads[:3]:
        load.wait()
    for t in range(CT):
        tbl[t] = jnp.concatenate([st[:, t * 128 : (t + 1) * 128], jnp.zeros((3, 128), F32)], axis=0)
    own = [tbl[t] for t in range(CT)]
    near_ids = []
    for b in range(BITS):
        row = sd[pl.ds(beside[b], 1), :]
        near_ids.append(wide(jnp.concatenate([row, row], axis=1)))
    far_ids = [wide(gi[i : i + 1, :]) for i in range(2)]
    for i, ids in enumerate(near_ids + far_ids):
        snd1[i] = selected(own, ids & 127, ids >> 7, 0, None)

    first = exchange(
        snd1, rcv1, lambda i: snd1.at[BITS + i], lambda i: rcv1.at[BITS + i], s1, r1
    )
    second = exchange(snd2, rcv2, lambda i: snd3.at[i], lambda i: rcv3.at[i], s2, r2)
    pl.semaphore_wait(barrier, BITS + jnp.where(has_low, 1, 0) + jnp.where(has_high, 1, 0))
    start(*first)

    @pl.when(g == 0)
    def _():
        rcv1[BITS] = jnp.zeros((8, 128), F32)
        rcv3[0] = jnp.zeros((7, 8, 128), F32)

    @pl.when(g == groups - 1)
    def _():
        rcv1[BITS + 1] = jnp.zeros((8, 128), F32)
        rcv3[1] = jnp.zeros((7, 8, 128), F32)

    loads[3].wait()

    def own_neighbours(ct):
        for jt in range(JT):
            index = table_index(sn[jt * 8 : jt * 8 + 8, lanes_at(ct)], d)
            nidx[ct, jt] = index
            lanes, tile = index & 127, index >> 7
            for v in range(5):
                tiles = [wide(tbl[t, v : v + 1, :]) for t in range(CT)]
                near[ct, v, jt] = selected(tiles, lanes, tile, 0, None)

    loop(CT, own_neighbours)
    loads[4].wait()

    def widen(ct):
        for k in range(COEF):
            pf[ct, k] = pb[k, :, lanes_at(ct)].astype(F32)

    loop(CT, widen)

    received(*first)
    tbl[6] = jnp.where(lower_half, rcv1[0], rcv1[1])
    tbl[7] = jnp.where(lower_half, rcv1[2], rcv1[3])
    tbl[8] = rcv1[4]
    tbl[9] = rcv1[5]
    tbl[10] = rcv1[6]

    def coefficients(ct):
        diffs = [[None] * JT for _ in range(5)]
        for jt in range(JT):
            index = nidx[ct, jt]
            lanes, tile = index & 127, index >> 7
            for v in range(5):
                tiles = [wide(tbl[t, v : v + 1, :]) for t in range(CT, 11)]
                value = selected(tiles, lanes, tile, CT, near[ct, v, jt])
                diff = value - wide(tbl[ct, v : v + 1, :])
                diffs[v][jt] = diff.astype(BF16).astype(F32)
        for r in range(ROWS):
            parts = []
            for s in range(8):
                v, k = divmod(8 * r + s, COEF)
                if v > 4:
                    parts.append(jnp.zeros((8, 128), F32))
                    continue
                acc = None
                for jt in range(JT):
                    term = pf[ct, k, jt * 8 : jt * 8 + 8, :] * diffs[v][jt]
                    acc = term if acc is None else acc + term
                parts.append(acc)
            ctab[r, ct] = row_sums(parts)

    loop(CT, coefficients)

    spread = [lane_gather(ids, lane & 31) for ids in near_ids]
    mixed = spread[0]
    for q in range(1, 4):
        mixed = jnp.where(quarter == q, spread[q], mixed)
    turned = [mixed] + [pltpu.roll(mixed, 32 * a, 1) for a in range(1, 4)]
    ends = jnp.where(lower_half, far_ids[0], pltpu.roll(far_ids[1], 64, 1))
    ends = [ends, pltpu.roll(ends, 64, 1)]

    def picked(r, ids):
        return selected([ctab[r, t] for t in range(CT)], ids & 127, ids >> 7, 0, None)

    for m in range(4):
        rows = range(4 * m, min(4 * m + 4, ROWS))
        got = [picked(r, turned[r % 4]) for r in rows]
        last = [picked(r, spread[4]) for r in rows]
        if len(got) == 1:
            for b in range(4):
                snd2[b, m] = got[0]
            snd2[4, m] = last[0]
            continue
        for b in range(4):
            mix = got[-b % 4]
            for q in range(1, 4):
                mix = jnp.where(quarter == q, got[(q - b) % 4], mix)
            snd2[b, m] = mix
        mix = last[0]
        for q in range(1, 4):
            mix = jnp.where(quarter == q, last[q], mix)
        snd2[4, m] = mix
    for m in range(7):
        rows = range(2 * m, min(2 * m + 2, ROWS))
        got = [picked(r, ends[r % 2]) for r in rows]
        snd3[0, m] = jnp.where(lower_half, got[0], got[-1])
        snd3[1, m] = jnp.where(lower_half, got[-1], got[0])
    start(*second)

    for load in loads[5:]:
        load.wait()

    def unpack_basis(ft):
        at = lanes_at(ft)
        bf32[ft] = fb[:, at].astype(F32)
        for i in range(4):
            base = 20 * i
            bas[i, 0, ft] = bf32[ft, base : base + 8, :]
            bas[i, 1, ft] = bf32[ft, base + 8 : base + 16, :]
            bas[i, 2, ft] = jnp.concatenate(
                [bf32[ft, base + 16 : base + 20, :], bf32[ft, base : base + 4, :]], axis=0
            )
            bas[i, 3, ft] = bf32[ft, base + 4 : base + 12, :]
            bas[i, 4, ft] = bf32[ft, base + 12 : base + 20, :]

    loop(FT, unpack_basis)

    def left_side(ft):
        slot = wide(fc[0:1, lanes_at(ft)])
        lanes, tile = slot & 127, slot >> 7
        coefs = [
            selected([ctab[r, t] for t in range(CT)], lanes, tile, 0, None) for r in range(ROWS)
        ]
        polynomials(coefs, 0, ft, bas, part)

    loop(FT, left_side)

    def right_own(ft):
        slot = wide(fc[1:2, lanes_at(ft)])
        lanes, tile = slot & 127, slot >> 7
        for r in range(ROWS):
            rgat[ft, r] = selected([ctab[r, t] for t in range(CT)], lanes, tile, 0, None)

    loop(FT, right_own)

    for ft in range(FT):
        at = slice(ft * 128, ft * 128 + 128)
        for i in range(2):
            row = i * 4 + ft % 4
            for e in range(2):
                slots[e, ft // 4, row : row + 1, :] = fc[e : e + 1, at]
            for e in range(4):
                geo[e, ft // 4, row : row + 1, :] = fg[e : e + 1, at]

    def centres(u):
        slot = slots[0, u]
        for v in range(5):
            tiles = [wide(tbl[t, v : v + 1, :]) for t in range(CT)]
            cen[0, v, u] = selected(tiles, slot & 127, slot >> 7, 0, None)
        index = table_index(slots[1, u], d)
        for v in range(5):
            tiles = [wide(tbl[t, v : v + 1, :]) for t in range(11)]
            cen[1, v, u] = selected(tiles, index & 127, index >> 7, 0, None)
        for v in range(5):
            left_w[v, u] = cen[0, v, u] + row_sums([part[v, u * 8 + s] for s in range(8)])

    loop(UT, centres)

    def incidence(ft):
        at = lanes_at(ft)
        cell = lax.broadcasted_iota(I32, (CELLS, 128), 0)
        sign = jnp.where(
            cell == fc[0:1, at], 1.0, jnp.where(cell == fc[1:2, at], -1.0, 0.0)
        )
        inc[:, at] = sign.astype(BF16)

    loop(FT, incidence)

    received(*second)

    for r in range(ROWS):
        m, a = divmod(r, 4)
        mix = rcv2[-a % 4, m]
        for q in range(1, 4):
            mix = jnp.where(quarter == q, rcv2[(q - a) % 4, m], mix)
        gtab[r, 0] = mix
        gtab[r, 1] = jnp.where(lower_half, rcv3[r % 2, r // 2], rcv3[1 - r % 2, r // 2])
        gtab[r, 2] = rcv2[4, m]

    def right_side(ft):
        index = coef_index(wide(fc[1:2, lanes_at(ft)]), d)
        tile = index >> 7
        lanes = [(index + 32 * a) & 127 for a in range(4)]
        coefs = []
        for r in range(ROWS):
            acc = rgat[ft, r]
            for i, a in enumerate((r % 4, 2 * (r % 2), r % 4)):
                acc = selected([gtab[r, i]], lanes[a], tile, CT + i, acc)
            coefs.append(acc)
        polynomials(coefs, 1, ft, bas, part)

    loop(FT, right_side)

    wrow[...] = jnp.zeros((FT, 8, 128), F32)

    def fluxes(u):
        left = floored([left_w[v, u] for v in range(5)])
        right = [cen[1, v, u] + row_sums([part[v, u * 8 + s] for s in range(8)]) for v in range(5)]
        flux = roe_flux(left, floored(right), [geo[i, u] for i in range(3)])
        scale = 0.25 * geo[3, u]
        for v in range(5):
            weighted = scale * flux[v]
            weighted = weighted + pltpu.roll(weighted, 4, 0)
            for i in range(4):
                wrow[u * 4 + i, v : v + 1, :] = weighted[i : i + 1, :]

    loop(UT, fluxes)

    def split(ft):
        whole = wrow[ft]
        high = whole.astype(BF16).astype(F32)
        wl[:, lanes_at(ft)] = jnp.concatenate([high, whole - high], axis=0).astype(BF16)

    loop(FT, split)
    summed = lax.dot_general(
        wl[...], inc[...], (((1,), (1,)), ((), ())), preferred_element_type=F32
    )
    out_ref[...] = summed[0:5] + summed[8:13]
    sent(*first)
    sent(*second)


def per_device(groups, *args):
    any_spec = pl.BlockSpec(memory_space=pl.ANY)
    vmem = pltpu.VMEM
    tile = (8, 128)
    scratch = [
        vmem((5, CELLS), F32),
        vmem((COEF, STEN, CELLS), BF16),
        vmem((STEN, CELLS), I32),
        vmem(args[3].shape, I32),
        vmem((2, 128), I32),
        vmem((2, FACES), I32),
        vmem((4, FACES), F32),
        vmem((80, FACES), BF16),
        vmem((11,) + tile, F32),
        vmem((7,) + tile, F32),
        vmem((7,) + tile, F32),
        vmem((BITS, 4) + tile, F32),
        vmem((BITS, 4) + tile, F32),
        vmem((2, 7) + tile, F32),
        vmem((2, 7) + tile, F32),
        vmem((CT, JT) + tile, I32),
        vmem((CT, COEF, STEN, 128), F32),
        vmem((CT, 5, JT) + tile, F32),
        vmem((ROWS, CT) + tile, F32),
        vmem((FT, ROWS) + tile, F32),
        vmem((ROWS, 3) + tile, F32),
        vmem((4, 5, FT) + tile, F32),
        vmem((FT, 80, 128), F32),
        vmem((CELLS, FACES), BF16),
        vmem((2, UT) + tile, I32),
        vmem((4, UT) + tile, F32),
        vmem((5, 2 * FT) + tile, F32),
        vmem((2, 5, UT) + tile, F32),
        vmem((5, UT) + tile, F32),
        vmem((FT,) + tile, F32),
        vmem((16, FACES), BF16),
        pltpu.SemaphoreType.DMA((8,)),
        pltpu.SemaphoreType.DMA((7,)),
        pltpu.SemaphoreType.DMA((7,)),
        pltpu.SemaphoreType.DMA((7,)),
        pltpu.SemaphoreType.DMA((7,)),
    ]
    return pl.pallas_call(
        functools.partial(kernel, groups),
        out_shape=jax.ShapeDtypeStruct((5, CELLS), F32),
        in_specs=[any_spec] * 8,
        out_specs=pl.BlockSpec(memory_space=pltpu.VMEM),
        scratch_shapes=scratch,
        compiler_params=pltpu.CompilerParams(
            collective_id=0, has_side_effects=True, vmem_limit_bytes=56 * 1024 * 1024
        ),
    )(*args)


def solution(mesh):
    both = ("group", "dom")
    in_specs = (
        P(None, both),
        P(None, None, both),
        P(None, both),
        P(both, None),
        P(both, None),
        P(None, both),
        P(None, both),
        P(None, both),
    )
    return jax.shard_map(
        functools.partial(per_device, mesh.shape["group"]),
        mesh=mesh,
        in_specs=in_specs,
        out_specs=P(None, both),
        check_vma=False,
    )
```

time: 223 us -> 25.2 us (0.11)
  the two profiles are of different devices: /device:TPU:195 before, /device:TPU:199 now
where the time goes in v1:
time: 25.2 us; the launch traced here: 25 us
  Pallas kernels  23.7 us (94%)
  local copies, waits for them, and re-layouts  1.35 us (5%)
    pallas_call x1, Pallas kernels, per_device(): pl.pallas_call(functools.partial(kernel, groups), out_shape=jax.ShapeDtyp...  23.7 us
    unnamed x1, local copies, waits for them, and re-layouts  1.35 us

profile of v1, /device:TPU:199, one launch (start us, length us, event | category | flops | bytes accessed | tf_op | source)
XLA Modules:
  0.0 25.0 jit_solution(16903359378218460198)
XLA Ops:
  0.0 23.7 %shard_map.82 = f32[5,768]{1,0:T(8,128)} custom-call(f32[5,768]{1,0:T(8,128)} %state_h.1, bf16[20,40,768]{2,1,0:T(8,128)(2,1)} %pinv_h.1, s32[40,768]{1,0:T(8,128)} %sten_h.1, s32[32,64]{1,0:T(8,128)} %send_h.1, s32[2,128]{1,0:T(2,128)} %gids_h.1, s32[2,1536]{1,0:T(2,128)} %fc_h.1, f32[4,1536]{1,0:T(4,128)} %fg_h.1, bf16[80,1536]{1,0:T(8,128)(2,1)} %fb_h.1), custom_call_target="tpu_custom_call" | custom-call | tf_op jit(solution)/shard_map/pallas_call | solution.py:537
  23.7 1.3 %copy.10 = f32[5,768]{1,0:T(8,128)} copy(f32[5,768]{1,0:T(8,128)} %shard_map.82) | data formatting | bytes 30720

commit v2 on v1

--- a/solution.py
+++ b/solution.py
@@ -23,6 +23,7 @@
 JT = STEN // 8
 ROWS = 13
 BITS = 5
+ORDER = (4, 1, 3, 0, 2)
 UT = FT // 4
 
 
@@ -50,17 +51,9 @@
     return lax.broadcasted_iota(I32, (8, 128), axis)
 
 
-def merged(first, second, distance):
-    mask = (iota(0) & distance) == 0
-    kept = jnp.where(mask, first, second)
-    moved = jnp.where(mask, second, first)
-    return kept + pltpu.roll(moved, distance, 0)
-
-
-def row_sums(parts):
-    for distance in (1, 2, 4):
-        parts = [merged(parts[i], parts[i + 1], distance) for i in range(0, len(parts), 2)]
-    return parts[0]
+def row_sums(ref):
+    x = [ref[pl.ds(j, 8, stride=8), :] for j in range(8)]
+    return ((x[0] + x[1]) + (x[2] + x[3])) + ((x[4] + x[5]) + (x[6] + x[7]))
 
 
 def selected(tiles, lanes, tile, start, acc):
@@ -153,21 +146,21 @@
     return [jnp.maximum(w[0], FLOOR), w[1], w[2], w[3], jnp.maximum(w[4], FLOOR)]
 
 
-def polynomials(coefs, side, tile, basis, part):
+def polynomials(coefs, side, u, f, basis, part):
     low = iota(0) < 4
-    place = (tile // 4) * 8 + tile % 4
     for point in range(2):
-        terms = [coefs[r] * basis[side * 2 + point, r % 5, tile] for r in range(ROWS)]
+        terms = [coefs[r] * basis[side * 2 + point, r % 5, u * 4 + f] for r in range(ROWS)]
         split = {r: (jnp.where(low, terms[r], 0.0), jnp.where(low, 0.0, terms[r])) for r in (2, 7)}
         sums = [
-            terms[0] + terms[1] + split[2][0],
-            split[2][1] + terms[3] + terms[4],
-            terms[5] + terms[6] + split[7][0],
-            split[7][1] + terms[8] + terms[9],
-            terms[10] + terms[11] + jnp.where(low, terms[12], 0.0),
+            (terms[0] + terms[1]) + split[2][0],
+            (terms[3] + terms[4]) + split[2][1],
+            (terms[5] + terms[6]) + split[7][0],
+            (terms[8] + terms[9]) + split[7][1],
+            (terms[10] + terms[11]) + jnp.where(low, terms[12], 0.0),
         ]
+        place = (point * 4 + f) * 8
         for v in range(5):
-            part[v, place + 4 * point] = sums[v]
+            part[v, u, place : place + 8, :] = sums[v]
 
 
 def kernel(
@@ -176,8 +169,8 @@
     out_ref,
     st, pb, sn, sd, gi, fc, fg, fb,
     tbl, snd1, rcv1, snd2, rcv2, snd3, rcv3,
-    nidx, pf, near, ctab, rgat, gtab, bas, bf32, inc, slots, geo,
-    part, cen, left_w, wrow, wl,
+    nidx, ridx, pf, near, ctab, rgat, gtab, bas, bf32, hot, slots, geo,
+    part, terms, cen, left_w, turn, wl,
     in_sem, s1, r1, s2, r2,
 ):
     g = lax.axis_index("group")
@@ -186,22 +179,22 @@
     has_low = g > 0
     has_high = g < groups - 1
 
+    barrier = pltpu.get_barrier_semaphore()
+    for b in ORDER:
+        pl.semaphore_signal(barrier, inc=1, device_id=(g, beside[b]), device_id_type=MESH)
+
+    @pl.when(has_low)
+    def _():
+        pl.semaphore_signal(barrier, inc=1, device_id=(g - 1, d), device_id_type=MESH)
+
+    @pl.when(has_high)
+    def _():
+        pl.semaphore_signal(barrier, inc=1, device_id=(g + 1, d), device_id_type=MESH)
+
     pairs = [(state_h, st), (send_h, sd), (gids_h, gi), (sten_h, sn), (pinv_h, pb), (fc_h, fc), (fb_h, fb), (fg_h, fg)]
     loads = [pltpu.make_async_copy(a, b, in_sem.at[i]) for i, (a, b) in enumerate(pairs)]
     for load in loads:
         load.start()
-
-    barrier = pltpu.get_barrier_semaphore()
-    for b in range(BITS):
-        pl.semaphore_signal(barrier, inc=1, device_id=(g, beside[b]), device_id_type=MESH)
-
-    @pl.when(has_low)
-    def _():
-        pl.semaphore_signal(barrier, inc=1, device_id=(g - 1, d), device_id_type=MESH)
-
-    @pl.when(has_high)
-    def _():
-        pl.semaphore_signal(barrier, inc=1, device_id=(g + 1, d), device_id_type=MESH)
 
     def exchange(near_src, near_dst, far_src, far_dst, send, recv):
         copies = [
@@ -228,15 +221,13 @@
         ]
         return copies, up, down
 
-    def start(copies, up, down):
-        for b in reversed(range(BITS)):
-            copies[b].start()
+    def start_far(copies, up, down):
         pl.when(has_high)(up.start)
         pl.when(has_low)(down.start)
 
     def received(copies, up, down):
-        for copy in copies:
-            copy.wait_recv()
+        for b in reversed(ORDER[1:]):
+            copies[b].wait_recv()
         pl.when(has_low)(up.wait_recv)
         pl.when(has_high)(down.wait_recv)
 
@@ -268,7 +259,9 @@
     )
     second = exchange(snd2, rcv2, lambda i: snd3.at[i], lambda i: rcv3.at[i], s2, r2)
     pl.semaphore_wait(barrier, BITS + jnp.where(has_low, 1, 0) + jnp.where(has_high, 1, 0))
-    start(*first)
+    for b in ORDER:
+        first[0][b].start()
+    start_far(*first)
 
     @pl.when(g == 0)
     def _():
@@ -292,85 +285,14 @@
                 near[ct, v, jt] = selected(tiles, lanes, tile, 0, None)
 
     loop(CT, own_neighbours)
-    loads[4].wait()
+    for load in loads[4:]:
+        load.wait()
 
     def widen(ct):
         for k in range(COEF):
             pf[ct, k] = pb[k, :, lanes_at(ct)].astype(F32)
 
     loop(CT, widen)
-
-    received(*first)
-    tbl[6] = jnp.where(lower_half, rcv1[0], rcv1[1])
-    tbl[7] = jnp.where(lower_half, rcv1[2], rcv1[3])
-    tbl[8] = rcv1[4]
-    tbl[9] = rcv1[5]
-    tbl[10] = rcv1[6]
-
-    def coefficients(ct):
-        diffs = [[None] * JT for _ in range(5)]
-        for jt in range(JT):
-            index = nidx[ct, jt]
-            lanes, tile = index & 127, index >> 7
-            for v in range(5):
-                tiles = [wide(tbl[t, v : v + 1, :]) for t in range(CT, 11)]
-                value = selected(tiles, lanes, tile, CT, near[ct, v, jt])
-                diff = value - wide(tbl[ct, v : v + 1, :])
-                diffs[v][jt] = diff.astype(BF16).astype(F32)
-        for r in range(ROWS):
-            parts = []
-            for s in range(8):
-                v, k = divmod(8 * r + s, COEF)
-                if v > 4:
-                    parts.append(jnp.zeros((8, 128), F32))
-                    continue
-                acc = None
-                for jt in range(JT):
-                    term = pf[ct, k, jt * 8 : jt * 8 + 8, :] * diffs[v][jt]
-                    acc = term if acc is None else acc + term
-                parts.append(acc)
-            ctab[r, ct] = row_sums(parts)
-
-    loop(CT, coefficients)
-
-    spread = [lane_gather(ids, lane & 31) for ids in near_ids]
-    mixed = spread[0]
-    for q in range(1, 4):
-        mixed = jnp.where(quarter == q, spread[q], mixed)
-    turned = [mixed] + [pltpu.roll(mixed, 32 * a, 1) for a in range(1, 4)]
-    ends = jnp.where(lower_half, far_ids[0], pltpu.roll(far_ids[1], 64, 1))
-    ends = [ends, pltpu.roll(ends, 64, 1)]
-
-    def picked(r, ids):
-        return selected([ctab[r, t] for t in range(CT)], ids & 127, ids >> 7, 0, None)
-
-    for m in range(4):
-        rows = range(4 * m, min(4 * m + 4, ROWS))
-        got = [picked(r, turned[r % 4]) for r in rows]
-        last = [picked(r, spread[4]) for r in rows]
-        if len(got) == 1:
-            for b in range(4):
-                snd2[b, m] = got[0]
-            snd2[4, m] = last[0]
-            continue
-        for b in range(4):
-            mix = got[-b % 4]
-            for q in range(1, 4):
-                mix = jnp.where(quarter == q, got[(q - b) % 4], mix)
-            snd2[b, m] = mix
-        mix = last[0]
-        for q in range(1, 4):
-            mix = jnp.where(quarter == q, last[q], mix)
-        snd2[4, m] = mix
-    for m in range(7):
-        rows = range(2 * m, min(2 * m + 2, ROWS))
-        got = [picked(r, ends[r % 2]) for r in rows]
-        snd3[0, m] = jnp.where(lower_half, got[0], got[-1])
-        snd3[1, m] = jnp.where(lower_half, got[-1], got[0])
-    start(*second)
-
-    for load in loads[5:]:
-        load.wait()
 
     def unpack_basis(ft):
         at = lanes_at(ft)
@@ -384,26 +306,13 @@
             )
             bas[i, 3, ft] = bf32[ft, base + 4 : base + 12, :]
             bas[i, 4, ft] = bf32[ft, base + 12 : base + 20, :]
+        cell = lax.broadcasted_iota(I32, (128, 128), 0)
+        for e in range(2):
+            same = cell == (fc[e : e + 1, at] & 127)
+            hot[e * 128 : e * 128 + 128, at] = jnp.where(same, 1.0, 0.0).astype(BF16)
+        ridx[ft] = coef_index(wide(fc[1:2, at]), d)
 
     loop(FT, unpack_basis)
-
-    def left_side(ft):
-        slot = wide(fc[0:1, lanes_at(ft)])
-        lanes, tile = slot & 127, slot >> 7
-        coefs = [
-            selected([ctab[r, t] for t in range(CT)], lanes, tile, 0, None) for r in range(ROWS)
-        ]
-        polynomials(coefs, 0, ft, bas, part)
-
-    loop(FT, left_side)
-
-    def right_own(ft):
-        slot = wide(fc[1:2, lanes_at(ft)])
-        lanes, tile = slot & 127, slot >> 7
-        for r in range(ROWS):
-            rgat[ft, r] = selected([ctab[r, t] for t in range(CT)], lanes, tile, 0, None)
-
-    loop(FT, right_own)
 
     for ft in range(FT):
         at = slice(ft * 128, ft * 128 + 128)
@@ -414,29 +323,120 @@
             for e in range(4):
                 geo[e, ft // 4, row : row + 1, :] = fg[e : e + 1, at]
 
+    received(*first)
+    tbl[6] = jnp.where(lower_half, rcv1[0], rcv1[1])
+    tbl[7] = jnp.where(lower_half, rcv1[2], rcv1[3])
+    tbl[9] = rcv1[5]
+    tbl[10] = rcv1[6]
+
+    def other_neighbours(ct):
+        for jt in range(JT):
+            index = nidx[ct, jt]
+            lanes, tile = index & 127, index >> 7
+            for v in range(5):
+                acc = near[ct, v, jt]
+                for t in (6, 7, 9, 10):
+                    acc = selected([wide(tbl[t, v : v + 1, :])], lanes, tile, t, acc)
+                near[ct, v, jt] = acc
+
+    for i in range(6): other_neighbours(i)
+
+    first[0][4].wait_recv()
+    tbl[8] = rcv1[4]
+
+    def coefficients(pair):
+        for i in range(6):
+            ct = i
+            diffs = [[None] * JT for _ in range(5)]
+            for jt in range(JT):
+                index = nidx[ct, jt]
+                lanes, tile = index & 127, index >> 7
+                for v in range(5):
+                    value = selected([wide(tbl[8, v : v + 1, :])], lanes, tile, 8, near[ct, v, jt])
+                    diff = value - wide(tbl[ct, v : v + 1, :])
+                    diffs[v][jt] = diff.astype(BF16).astype(F32)
+            for r in range(ROWS):
+                for s in range(8):
+                    v, k = divmod(8 * r + s, COEF)
+                    if v > 4:
+                        continue
+                    x = [pf[ct, k, jt * 8 : jt * 8 + 8, :] * diffs[v][jt] for jt in range(JT)]
+                    terms[i, r, s * 8 : s * 8 + 8, :] = ((x[0] + x[1]) + (x[2] + x[3])) + x[4]
+            for r in range(ROWS):
+                ctab[r, ct] = row_sums(terms.at[i, r])
+
+    terms[:, ROWS - 1, 32:64, :] = jnp.zeros((6, 32, 128), F32)
+    coefficients(0)
+
+    spread = [lane_gather(ids, lane & 31) for ids in near_ids]
+    mixed = spread[0]
+    for q in range(1, 4):
+        mixed = jnp.where(quarter == q, spread[q], mixed)
+    turned = [mixed] + [pltpu.roll(mixed, 32 * a, 1) for a in range(1, 4)]
+    ends = jnp.where(lower_half, far_ids[0], pltpu.roll(far_ids[1], 64, 1))
+    ends = [ends, pltpu.roll(ends, 64, 1)]
+
+    def picked(r, ids):
+        return selected([ctab[r, t] for t in range(CT)], ids & 127, ids >> 7, 0, None)
+
+    groups_of = [range(4 * m, min(4 * m + 4, ROWS)) for m in range(4)]
+    for m, rows in enumerate(groups_of):
+        got = [picked(r, spread[4]) for r in rows]
+        mix = got[0]
+        for q in range(1, len(got)):
+            mix = jnp.where(quarter == q, got[q], mix)
+        snd2[4, m] = mix
+    second[0][4].start()
+    for m, rows in enumerate(groups_of):
+        got = [picked(r, turned[r % 4]) for r in rows]
+        for b in range(4):
+            mix = got[-b % len(got)]
+            for q in range(1, len(got)):
+                mix = jnp.where(quarter == q, got[(q - b) % 4], mix)
+            snd2[b, m] = mix
+    for b in ORDER[1:]:
+        second[0][b].start()
+    for m in range(7):
+        rows = range(2 * m, min(2 * m + 2, ROWS))
+        got = [picked(r, ends[r % 2]) for r in rows]
+        snd3[0, m] = jnp.where(lower_half, got[0], got[-1])
+        snd3[1, m] = jnp.where(lower_half, got[-1], got[0])
+    start_far(*second)
+
+    def left_side(u):
+        for f in range(4):
+            slot = wide(fc[0:1, lanes_at(u * 4 + f)])
+            lanes, tile = slot & 127, slot >> 7
+            coefs = [
+                selected([ctab[r, t] for t in range(CT)], lanes, tile, 0, None)
+                for r in range(ROWS)
+            ]
+            polynomials(coefs, 0, u, f, bas, part)
+
+    loop(UT, left_side)
+
+    def right_own(u):
+        for f in range(4):
+            index = ridx[u * 4 + f]
+            lanes, tile = index & 127, index >> 7
+            for r in range(ROWS):
+                own_part = selected([ctab[r, t] for t in range(CT)], lanes, tile, 0, None)
+                rgat[u * 4 + f, r] = own_part
+
+    loop(UT, right_own)
+
     def centres(u):
         slot = slots[0, u]
         for v in range(5):
             tiles = [wide(tbl[t, v : v + 1, :]) for t in range(CT)]
-            cen[0, v, u] = selected(tiles, slot & 127, slot >> 7, 0, None)
+            centre = selected(tiles, slot & 127, slot >> 7, 0, None)
+            left_w[v, u] = centre + row_sums(part.at[v, u])
         index = table_index(slots[1, u], d)
         for v in range(5):
             tiles = [wide(tbl[t, v : v + 1, :]) for t in range(11)]
-            cen[1, v, u] = selected(tiles, index & 127, index >> 7, 0, None)
-        for v in range(5):
-            left_w[v, u] = cen[0, v, u] + row_sums([part[v, u * 8 + s] for s in range(8)])
+            cen[v, u] = selected(tiles, index & 127, index >> 7, 0, None)
 
     loop(UT, centres)
-
-    def incidence(ft):
-        at = lanes_at(ft)
-        cell = lax.broadcasted_iota(I32, (CELLS, 128), 0)
-        sign = jnp.where(
-            cell == fc[0:1, at], 1.0, jnp.where(cell == fc[1:2, at], -1.0, 0.0)
-        )
-        inc[:, at] = sign.astype(BF16)
-
-    loop(FT, incidence)
 
     received(*second)
 
@@ -447,47 +447,61 @@
             mix = jnp.where(quarter == q, rcv2[(q - a) % 4, m], mix)
         gtab[r, 0] = mix
         gtab[r, 1] = jnp.where(lower_half, rcv3[r % 2, r // 2], rcv3[1 - r % 2, r // 2])
-        gtab[r, 2] = rcv2[4, m]
-
-    def right_side(ft):
-        index = coef_index(wide(fc[1:2, lanes_at(ft)]), d)
-        tile = index >> 7
-        lanes = [(index + 32 * a) & 127 for a in range(4)]
-        coefs = []
-        for r in range(ROWS):
-            acc = rgat[ft, r]
-            for i, a in enumerate((r % 4, 2 * (r % 2), r % 4)):
-                acc = selected([gtab[r, i]], lanes[a], tile, CT + i, acc)
-            coefs.append(acc)
-        polynomials(coefs, 1, ft, bas, part)
-
-    loop(FT, right_side)
-
-    wrow[...] = jnp.zeros((FT, 8, 128), F32)
-
-    def fluxes(u):
+
+    def right_near(u):
+        for f in range(4):
+            index = ridx[u * 4 + f]
+            tile = index >> 7
+            lanes = [(index + 32 * a) & 127 for a in range(4)]
+            for r in range(ROWS):
+                acc = rgat[u * 4 + f, r]
+                acc = selected([gtab[r, 0]], lanes[r % 4], tile, 6, acc)
+                rgat[u * 4 + f, r] = selected([gtab[r, 1]], lanes[2 * (r % 2)], tile, 7, acc)
+
+    for u in range(UT): right_near(u)
+    turn[...] = jnp.zeros((UT, 64, 128), F32)
+    second[0][4].wait_recv()
+
+    total = None
+    for u in range(UT):
+        for f in range(4):
+            index = ridx[u * 4 + f]
+            tile = index >> 7
+            lanes = [(index + 32 * a) & 127 for a in range(4)]
+            coefs = [
+                selected([rcv2[4, r // 4]], lanes[r % 4], tile, 8, rgat[u * 4 + f, r])
+                for r in range(ROWS)
+            ]
+            polynomials(coefs, 1, u, f, bas, part)
         left = floored([left_w[v, u] for v in range(5)])
-        right = [cen[1, v, u] + row_sums([part[v, u * 8 + s] for s in range(8)]) for v in range(5)]
-        flux = roe_flux(left, floored(right), [geo[i, u] for i in range(3)])
+        right = floored([cen[v, u] + row_sums(part.at[v, u]) for v in range(5)])
+        flux = roe_flux(left, right, [geo[i, u] for i in range(3)])
         scale = 0.25 * geo[3, u]
         for v in range(5):
             weighted = scale * flux[v]
-            weighted = weighted + pltpu.roll(weighted, 4, 0)
-            for i in range(4):
-                wrow[u * 4 + i, v : v + 1, :] = weighted[i : i + 1, :]
-
-    loop(UT, fluxes)
-
-    def split(ft):
-        whole = wrow[ft]
-        high = whole.astype(BF16).astype(F32)
-        wl[:, lanes_at(ft)] = jnp.concatenate([high, whole - high], axis=0).astype(BF16)
-
-    loop(FT, split)
-    summed = lax.dot_general(
-        wl[...], inc[...], (((1,), (1,)), ((), ())), preferred_element_type=F32
-    )
-    out_ref[...] = summed[0:5] + summed[8:13]
+            turn[u, v * 8 : v * 8 + 8, :] = weighted + pltpu.roll(weighted, 4, 0)
+        for f in range(4):
+            at = slice((u * 4 + f) * 128, (u * 4 + f + 1) * 128)
+            whole = turn[u, pl.ds(f, 8, stride=8), :]
+            high = whole.astype(BF16).astype(F32)
+            rest = whole - high
+            for e in range(2):
+                tile = wide(fc[e : e + 1, at]) >> 7
+                for t in range(CT):
+                    mask = tile == t
+                    rows = [jnp.where(mask, high, 0.0), jnp.where(mask, rest, 0.0)]
+                    place = (e * CT + t) * 16
+                    wl[place : place + 16, at] = jnp.concatenate(rows, axis=0).astype(BF16)
+        at = slice(u * 512, u * 512 + 512)
+        summed = lax.dot_general(
+            wl[:, at], hot[:, at], (((1,), (1,)), ((), ())), preferred_element_type=F32
+        )
+        total = summed if total is None else total + summed
+    for t in range(CT):
+        gained = total[t * 16 : t * 16 + 16, 0:128]
+        lost = total[(CT + t) * 16 : (CT + t) * 16 + 16, 128:256]
+        change = gained - lost
+        out_ref[:, t * 128 : t * 128 + 128] = (change[0:8] + change[8:16])[0:5]
     sent(*first)
     sent(*second)
 
@@ -513,21 +527,23 @@
         vmem((2, 7) + tile, F32),
         vmem((2, 7) + tile, F32),
         vmem((CT, JT) + tile, I32),
+        vmem((FT,) + tile, I32),
         vmem((CT, COEF, STEN, 128), F32),
         vmem((CT, 5, JT) + tile, F32),
         vmem((ROWS, CT) + tile, F32),
         vmem((FT, ROWS) + tile, F32),
-        vmem((ROWS, 3) + tile, F32),
+        vmem((ROWS, 2) + tile, F32),
         vmem((4, 5, FT) + tile, F32),
         vmem((FT, 80, 128), F32),
-        vmem((CELLS, FACES), BF16),
+        vmem((256, FACES), BF16),
         vmem((2, UT) + tile, I32),
         vmem((4, UT) + tile, F32),
-        vmem((5, 2 * FT) + tile, F32),
-        vmem((2, 5, UT) + tile, F32),
+        vmem((5, UT, 64, 128), F32),
+        vmem((6, ROWS, 64, 128), F32),
         vmem((5, UT) + tile, F32),
-        vmem((FT,) + tile, F32),
-        vmem((16, FACES), BF16),
+        vmem((5, UT) + tile, F32),
+        vmem((UT, 64, 128), F32),
+        vmem((192, FACES), BF16),
         pltpu.SemaphoreType.DMA((8,)),
         pltpu.SemaphoreType.DMA((7,)),
         pltpu.SemaphoreType.DMA((7,)),
@@ -536,7 +552,7 @@
     ]
     return pl.pallas_call(
         functools.partial(kernel, groups),
-        out_shape=jax.ShapeDtypeStruct((5, CELLS), F32),
+        out_shape=pltpu.VMEM((5, CELLS), F32),
         in_specs=[any_spec] * 8,
         out_specs=pl.BlockSpec(memory_space=pltpu.VMEM),
         scratch_shapes=scratch,

time: 25.2 us -> 21.9 us (0.87)
  the two profiles are of different devices: /device:TPU:199 before, /device:TPU:193 now
where the time goes in v2:
time: 21.9 us; the launch traced here: 21.8 us
  Pallas kernels  21.2 us (97%)
  local copies, waits for them, and re-layouts  0.61 us (3%)
    pallas_call x1, Pallas kernels, per_device(): pl.pallas_call(functools.partial(kernel, groups), out_shape=pltpu.VMEM((5...  21.2 us
    unnamed x1, local copies, waits for them, and re-layouts  0.61 us

profile of v2, /device:TPU:193, one launch (start us, length us, event | category | flops | bytes accessed | tf_op | source)
XLA Modules:
  0.0 21.8 jit_solution(12544560976492740078)
XLA Ops:
  0.0 21.2 %shard_map.82 = f32[5,768]{1,0:T(8,128)S(1)} custom-call(f32[5,768]{1,0:T(8,128)} %state_h.1, bf16[20,40,768]{2,1,0:T(8,128)(2,1)} %pinv_h.1, s32[40,768]{1,0:T(8,128)} %sten_h.1, s32[32,64]{1,0:T(8,128)} %send_h.1, s32[2,128]{1,0:T(2,128)} %gids_h.1, s32[2,1536]{1,0:T(2,128)} %fc_h.1, f32[4,1536]{1,0:T(4,128)} %fg_h.1, bf16[80,1536]{1,0:T(8,128)(2,1)} %fb_h.1), custom_call_target="tpu_custom_call" | custom-call | tf_op jit(solution)/shard_map/pallas_call | solution.py:553
  21.2 0.6 %copy.10 = f32[5,768]{1,0:T(8,128)} copy(f32[5,768]{1,0:T(8,128)S(1)} %shard_map.82) | data formatting | bytes 30720

commit v3 on v2

--- a/solution.py
+++ b/solution.py
@@ -25,6 +25,17 @@
 BITS = 5
 ORDER = (4, 1, 3, 0, 2)
 UT = FT // 4
+
+EARLY = ()
+LATE = (0, 1, 2, 3, 4, "ends")
+EARLY_COEFS = (0, 1, 2, 3, 4)
+LATE_COEFS = ("ends",)
+TABLE_TILES = {0: (6, 7), 4: (8,), "ends": (9, 10)}
+GHOST_TILES = {0: (0,), 4: (2,), "ends": (1,)}
+
+
+def tiles_of(kinds, tiles):
+    return [t for kind, of in tiles.items() if kind in kinds for t in of]
 
 
 def loop(count, body):
@@ -222,14 +233,16 @@
         return copies, up, down
 
     def start_far(copies, up, down):
+        pl.when(has_low)(down.start)
         pl.when(has_high)(up.start)
-        pl.when(has_low)(down.start)
-
-    def received(copies, up, down):
-        for b in reversed(ORDER[1:]):
-            copies[b].wait_recv()
-        pl.when(has_low)(up.wait_recv)
-        pl.when(has_high)(down.wait_recv)
+
+    def received(copies, up, down, kinds):
+        for kind in kinds:
+            if kind == "ends":
+                pl.when(has_low)(up.wait_recv)
+                pl.when(has_high)(down.wait_recv)
+            else:
+                copies[kind].wait_recv()
 
     def sent(copies, up, down):
         for copy in copies:
@@ -259,9 +272,10 @@
     )
     second = exchange(snd2, rcv2, lambda i: snd3.at[i], lambda i: rcv3.at[i], s2, r2)
     pl.semaphore_wait(barrier, BITS + jnp.where(has_low, 1, 0) + jnp.where(has_high, 1, 0))
-    for b in ORDER:
+    first[0][4].start()
+    start_far(*first)
+    for b in ORDER[1:]:
         first[0][b].start()
-    start_far(*first)
 
     @pl.when(g == 0)
     def _():
@@ -323,11 +337,18 @@
             for e in range(4):
                 geo[e, ft // 4, row : row + 1, :] = fg[e : e + 1, at]
 
-    received(*first)
-    tbl[6] = jnp.where(lower_half, rcv1[0], rcv1[1])
-    tbl[7] = jnp.where(lower_half, rcv1[2], rcv1[3])
-    tbl[9] = rcv1[5]
-    tbl[10] = rcv1[6]
+    def fill_table(kinds):
+        received(*first, kinds)
+        if 0 in kinds:
+            tbl[6] = jnp.where(lower_half, rcv1[0], rcv1[1])
+            tbl[7] = jnp.where(lower_half, rcv1[2], rcv1[3])
+        if 4 in kinds:
+            tbl[8] = rcv1[4]
+        if "ends" in kinds:
+            tbl[9] = rcv1[5]
+            tbl[10] = rcv1[6]
+
+    fill_table(EARLY)
 
     def other_neighbours(ct):
         for jt in range(JT):
@@ -335,14 +356,15 @@
             lanes, tile = index & 127, index >> 7
             for v in range(5):
                 acc = near[ct, v, jt]
-                for t in (6, 7, 9, 10):
+                for t in tiles_of(EARLY, TABLE_TILES):
                     acc = selected([wide(tbl[t, v : v + 1, :])], lanes, tile, t, acc)
                 near[ct, v, jt] = acc
 
-    for i in range(6): other_neighbours(i)
-
-    first[0][4].wait_recv()
-    tbl[8] = rcv1[4]
+    if EARLY:
+        for ct in range(CT):
+            other_neighbours(ct)
+
+    fill_table(LATE)
 
     def coefficients(pair):
         for i in range(6):
@@ -352,7 +374,9 @@
                 index = nidx[ct, jt]
                 lanes, tile = index & 127, index >> 7
                 for v in range(5):
-                    value = selected([wide(tbl[8, v : v + 1, :])], lanes, tile, 8, near[ct, v, jt])
+                    value = near[ct, v, jt]
+                    for t in tiles_of(LATE, TABLE_TILES):
+                        value = selected([wide(tbl[t, v : v + 1, :])], lanes, tile, t, value)
                     diff = value - wide(tbl[ct, v : v + 1, :])
                     diffs[v][jt] = diff.astype(BF16).astype(F32)
             for r in range(ROWS):
@@ -380,6 +404,12 @@
         return selected([ctab[r, t] for t in range(CT)], ids & 127, ids >> 7, 0, None)
 
     groups_of = [range(4 * m, min(4 * m + 4, ROWS)) for m in range(4)]
+    for m in range(7):
+        rows = range(2 * m, min(2 * m + 2, ROWS))
+        got = [picked(r, ends[r % 2]) for r in rows]
+        snd3[0, m] = jnp.where(lower_half, got[0], got[-1])
+        snd3[1, m] = jnp.where(lower_half, got[-1], got[0])
+    start_far(*second)
     for m, rows in enumerate(groups_of):
         got = [picked(r, spread[4]) for r in rows]
         mix = got[0]
@@ -396,12 +426,6 @@
             snd2[b, m] = mix
     for b in ORDER[1:]:
         second[0][b].start()
-    for m in range(7):
-        rows = range(2 * m, min(2 * m + 2, ROWS))
-        got = [picked(r, ends[r % 2]) for r in rows]
-        snd3[0, m] = jnp.where(lower_half, got[0], got[-1])
-        snd3[1, m] = jnp.where(lower_half, got[-1], got[0])
-    start_far(*second)
 
     def left_side(u):
         for f in range(4):
@@ -438,15 +462,29 @@
 
     loop(UT, centres)
 
-    received(*second)
-
-    for r in range(ROWS):
-        m, a = divmod(r, 4)
-        mix = rcv2[-a % 4, m]
-        for q in range(1, 4):
-            mix = jnp.where(quarter == q, rcv2[(q - a) % 4, m], mix)
-        gtab[r, 0] = mix
-        gtab[r, 1] = jnp.where(lower_half, rcv3[r % 2, r // 2], rcv3[1 - r % 2, r // 2])
+    def fill_ghosts(kinds):
+        received(*second, kinds)
+        for r in range(ROWS):
+            m, a = divmod(r, 4)
+            if 0 in kinds:
+                mix = rcv2[-a % 4, m]
+                for q in range(1, 4):
+                    mix = jnp.where(quarter == q, rcv2[(q - a) % 4, m], mix)
+                gtab[r, 0] = mix
+            if "ends" in kinds:
+                gtab[r, 1] = jnp.where(lower_half, rcv3[r % 2, r // 2], rcv3[1 - r % 2, r // 2])
+
+    def ghost_rows(kinds, lanes, tile, r, acc):
+        for t in tiles_of(kinds, GHOST_TILES):
+            if t == 0:
+                acc = selected([gtab[r, 0]], lanes[r % 4], tile, 6, acc)
+            elif t == 1:
+                acc = selected([gtab[r, 1]], lanes[2 * (r % 2)], tile, 7, acc)
+            else:
+                acc = selected([rcv2[4, r // 4]], lanes[r % 4], tile, 8, acc)
+        return acc
+
+    fill_ghosts(EARLY_COEFS)
 
     def right_near(u):
         for f in range(4):
@@ -455,48 +493,50 @@
             lanes = [(index + 32 * a) & 127 for a in range(4)]
             for r in range(ROWS):
                 acc = rgat[u * 4 + f, r]
-                acc = selected([gtab[r, 0]], lanes[r % 4], tile, 6, acc)
-                rgat[u * 4 + f, r] = selected([gtab[r, 1]], lanes[2 * (r % 2)], tile, 7, acc)
-
-    for u in range(UT): right_near(u)
+                rgat[u * 4 + f, r] = ghost_rows(EARLY_COEFS, lanes, tile, r, acc)
+
+    if EARLY_COEFS:
+        for u in range(UT):
+            right_near(u)
     turn[...] = jnp.zeros((UT, 64, 128), F32)
-    second[0][4].wait_recv()
-
-    total = None
+    fill_ghosts(LATE_COEFS)
+
     for u in range(UT):
         for f in range(4):
             index = ridx[u * 4 + f]
             tile = index >> 7
             lanes = [(index + 32 * a) & 127 for a in range(4)]
             coefs = [
-                selected([rcv2[4, r // 4]], lanes[r % 4], tile, 8, rgat[u * 4 + f, r])
+                ghost_rows(LATE_COEFS, lanes, tile, r, rgat[u * 4 + f, r])
                 for r in range(ROWS)
             ]
             polynomials(coefs, 1, u, f, bas, part)
-        left = floored([left_w[v, u] for v in range(5)])
-        right = floored([cen[v, u] + row_sums(part.at[v, u]) for v in range(5)])
-        flux = roe_flux(left, right, [geo[i, u] for i in range(3)])
-        scale = 0.25 * geo[3, u]
-        for v in range(5):
-            weighted = scale * flux[v]
-            turn[u, v * 8 : v * 8 + 8, :] = weighted + pltpu.roll(weighted, 4, 0)
-        for f in range(4):
-            at = slice((u * 4 + f) * 128, (u * 4 + f + 1) * 128)
-            whole = turn[u, pl.ds(f, 8, stride=8), :]
-            high = whole.astype(BF16).astype(F32)
-            rest = whole - high
-            for e in range(2):
-                tile = wide(fc[e : e + 1, at]) >> 7
-                for t in range(CT):
-                    mask = tile == t
-                    rows = [jnp.where(mask, high, 0.0), jnp.where(mask, rest, 0.0)]
-                    place = (e * CT + t) * 16
-                    wl[place : place + 16, at] = jnp.concatenate(rows, axis=0).astype(BF16)
-        at = slice(u * 512, u * 512 + 512)
-        summed = lax.dot_general(
-            wl[:, at], hot[:, at], (((1,), (1,)), ((), ())), preferred_element_type=F32
-        )
-        total = summed if total is None else total + summed
+    left = floored([left_w[v] for v in range(5)])
+    right = []
+    for v in range(5):
+        sums = [row_sums(part.at[v, u])[None] for u in range(UT)]
+        right.append(cen[v] + jnp.concatenate(sums, axis=0))
+    flux = roe_flux(left, floored(right), [geo[i] for i in range(3)])
+    scale = 0.25 * geo[3]
+    for v in range(5):
+        weighted = scale * flux[v]
+        for u in range(UT):
+            turn[u, v * 8 : v * 8 + 8, :] = weighted[u] + pltpu.roll(weighted[u], 4, 0)
+    for ft in range(FT):
+        at = slice(ft * 128, (ft + 1) * 128)
+        whole = turn[ft // 4, pl.ds(ft % 4, 8, stride=8), :]
+        high = whole.astype(BF16).astype(F32)
+        rest = whole - high
+        for e in range(2):
+            tile = wide(fc[e : e + 1, at]) >> 7
+            for t in range(CT):
+                mask = tile == t
+                rows = [jnp.where(mask, high, 0.0), jnp.where(mask, rest, 0.0)]
+                place = (e * CT + t) * 16
+                wl[place : place + 16, at] = jnp.concatenate(rows, axis=0).astype(BF16)
+    total = lax.dot_general(
+        wl[...], hot[...], (((1,), (1,)), ((), ())), preferred_element_type=F32
+    )
     for t in range(CT):
         gained = total[t * 16 : t * 16 + 16, 0:128]
         lost = total[(CT + t) * 16 : (CT + t) * 16 + 16, 128:256]

time: 21.9 us -> 21 us (0.959)
  the two profiles are of different devices: /device:TPU:193 before, /device:TPU:8 now
where the time goes in v3:
time: 21 us; the launch traced here: 20.9 us
  Pallas kernels  20.2 us (96%)
  local copies, waits for them, and re-layouts  0.61 us (3%)
    pallas_call x1, Pallas kernels, per_device(): pl.pallas_call(functools.partial(kernel, groups), out_shape=pltpu.VMEM((5...  20.2 us
    unnamed x1, local copies, waits for them, and re-layouts  0.61 us

profile of v3, /device:TPU:8, one launch (start us, length us, event | category | flops | bytes accessed | tf_op | source)
XLA Modules:
  0.0 20.9 jit_solution(6442623519856746859)
XLA Ops:
  0.0 20.2 %shard_map.82 = f32[5,768]{1,0:T(8,128)S(1)} custom-call(f32[5,768]{1,0:T(8,128)} %state_h.1, bf16[20,40,768]{2,1,0:T(8,128)(2,1)} %pinv_h.1, s32[40,768]{1,0:T(8,128)} %sten_h.1, s32[32,64]{1,0:T(8,128)} %send_h.1, s32[2,128]{1,0:T(2,128)} %gids_h.1, s32[2,1536]{1,0:T(2,128)} %fc_h.1, f32[4,1536]{1,0:T(4,128)} %fg_h.1, bf16[80,1536]{1,0:T(8,128)(2,1)} %fb_h.1), custom_call_target="tpu_custom_call" | custom-call | tf_op jit(solution)/shard_map/pallas_call | solution.py:593
  20.2 0.6 %copy.10 = f32[5,768]{1,0:T(8,128)} copy(f32[5,768]{1,0:T(8,128)S(1)} %shard_map.82) | data formatting | bytes 30720

commit v4 on v3

--- a/solution.py
+++ b/solution.py
@@ -26,11 +26,9 @@
 ORDER = (4, 1, 3, 0, 2)
 UT = FT // 4
 
-EARLY = ()
-LATE = (0, 1, 2, 3, 4, "ends")
+STATES = (0, 1, 2, 3, 4, "ends")
 EARLY_COEFS = (0, 1, 2, 3, 4)
 LATE_COEFS = ("ends",)
-TABLE_TILES = {0: (6, 7), 4: (8,), "ends": (9, 10)}
 GHOST_TILES = {0: (0,), 4: (2,), "ends": (1,)}
 
 
@@ -87,6 +85,22 @@
     near = jnp.where(bit < 4, 768 + bit * 32, 1024) + (slot & 31)
     far = 896 + jnp.where(slot < 2944, 0, 64) + (slot & 63)
     return jnp.where(slot < 768, slot, jnp.where(slot < 2816, near, far))
+
+
+def packed(tile):
+    row = iota(0)
+    lowest = jnp.where((row == 0) | (row == 4), 0.6, -0.5)
+    steps = ((tile - lowest) * 65535.0 + 0.5).astype(I32)
+    second = jnp.where(row == 0, pltpu.roll(steps, 4, 0), pltpu.roll(steps, 7, 0))
+    return steps | (second << 16)
+
+
+def low_half(word):
+    return word & 65535
+
+
+def high_half(word):
+    return lax.shift_right_logical(word, 16)
 
 
 def physical(w, n, vn):
@@ -179,8 +193,8 @@
     state_h, pinv_h, sten_h, send_h, gids_h, fc_h, fg_h, fb_h,
     out_ref,
     st, pb, sn, sd, gi, fc, fg, fb,
-    tbl, snd1, rcv1, snd2, rcv2, snd3, rcv3,
-    nidx, ridx, pf, near, ctab, rgat, gtab, bas, bf32, hot, slots, geo,
+    tbl, words, snd1, rcv1, snd2, rcv2, snd3, rcv3,
+    nidx, ridx, pf, near_words, near, ctab, rgat, gtab, bas, bf32, hot, slots, geo,
     part, terms, cen, left_w, turn, wl,
     in_sem, s1, r1, s2, r2,
 ):
@@ -289,14 +303,19 @@
 
     loads[3].wait()
 
+    for t in range(CT):
+        words[t] = packed(tbl[t])
+
     def own_neighbours(ct):
         for jt in range(JT):
             index = table_index(sn[jt * 8 : jt * 8 + 8, lanes_at(ct)], d)
             nidx[ct, jt] = index
             lanes, tile = index & 127, index >> 7
-            for v in range(5):
-                tiles = [wide(tbl[t, v : v + 1, :]) for t in range(CT)]
-                near[ct, v, jt] = selected(tiles, lanes, tile, 0, None)
+            for w in range(2):
+                tiles = [wide(words[t, w : w + 1, :]) for t in range(CT)]
+                near_words[ct, w, jt] = selected(tiles, lanes, tile, 0, None)
+            tiles = [wide(tbl[t, 3:4, :]) for t in range(CT)]
+            near[ct, jt] = selected(tiles, lanes, tile, 0, None)
 
     loop(CT, own_neighbours)
     for load in loads[4:]:
@@ -337,34 +356,14 @@
             for e in range(4):
                 geo[e, ft // 4, row : row + 1, :] = fg[e : e + 1, at]
 
-    def fill_table(kinds):
-        received(*first, kinds)
-        if 0 in kinds:
-            tbl[6] = jnp.where(lower_half, rcv1[0], rcv1[1])
-            tbl[7] = jnp.where(lower_half, rcv1[2], rcv1[3])
-        if 4 in kinds:
-            tbl[8] = rcv1[4]
-        if "ends" in kinds:
-            tbl[9] = rcv1[5]
-            tbl[10] = rcv1[6]
-
-    fill_table(EARLY)
-
-    def other_neighbours(ct):
-        for jt in range(JT):
-            index = nidx[ct, jt]
-            lanes, tile = index & 127, index >> 7
-            for v in range(5):
-                acc = near[ct, v, jt]
-                for t in tiles_of(EARLY, TABLE_TILES):
-                    acc = selected([wide(tbl[t, v : v + 1, :])], lanes, tile, t, acc)
-                near[ct, v, jt] = acc
-
-    if EARLY:
-        for ct in range(CT):
-            other_neighbours(ct)
-
-    fill_table(LATE)
+    received(*first, STATES)
+    tbl[6] = jnp.where(lower_half, rcv1[0], rcv1[1])
+    tbl[7] = jnp.where(lower_half, rcv1[2], rcv1[3])
+    tbl[8] = rcv1[4]
+    tbl[9] = rcv1[5]
+    tbl[10] = rcv1[6]
+    for t in range(CT, 11):
+        words[t] = packed(tbl[t])
 
     def coefficients(pair):
         for i in range(6):
@@ -373,12 +372,16 @@
             for jt in range(JT):
                 index = nidx[ct, jt]
                 lanes, tile = index & 127, index >> 7
-                for v in range(5):
-                    value = near[ct, v, jt]
-                    for t in tiles_of(LATE, TABLE_TILES):
-                        value = selected([wide(tbl[t, v : v + 1, :])], lanes, tile, t, value)
-                    diff = value - wide(tbl[ct, v : v + 1, :])
-                    diffs[v][jt] = diff.astype(BF16).astype(F32)
+                for w, (v_low, v_high) in enumerate(((0, 4), (1, 2))):
+                    tiles = [wide(words[t, w : w + 1, :]) for t in range(CT, 11)]
+                    word = selected(tiles, lanes, tile, CT, near_words[ct, w, jt])
+                    mine = wide(words[ct, w : w + 1, :])
+                    for v, unpack in ((v_low, low_half), (v_high, high_half)):
+                        steps = (unpack(word) - unpack(mine)).astype(F32)
+                        diffs[v][jt] = (steps * (1.0 / 65535.0)).astype(BF16).astype(F32)
+                tiles = [wide(tbl[t, 3:4, :]) for t in range(CT, 11)]
+                value = selected(tiles, lanes, tile, CT, near[ct, jt])
+                diffs[3][jt] = (value - wide(tbl[ct, 3:4, :])).astype(BF16).astype(F32)
             for r in range(ROWS):
                 for s in range(8):
                     v, k = divmod(8 * r + s, COEF)
@@ -560,6 +563,7 @@
         vmem((4, FACES), F32),
         vmem((80, FACES), BF16),
         vmem((11,) + tile, F32),
+        vmem((11,) + tile, I32),
         vmem((7,) + tile, F32),
         vmem((7,) + tile, F32),
         vmem((BITS, 4) + tile, F32),
@@ -569,7 +573,8 @@
         vmem((CT, JT) + tile, I32),
         vmem((FT,) + tile, I32),
         vmem((CT, COEF, STEN, 128), F32),
-        vmem((CT, 5, JT) + tile, F32),
+        vmem((CT, 2, JT) + tile, I32),
+        vmem((CT, JT) + tile, F32),
         vmem((ROWS, CT) + tile, F32),
         vmem((FT, ROWS) + tile, F32),
         vmem((ROWS, 2) + tile, F32),

time: 21 us -> 20.8 us (level)
  no operation moved by 1% of the time
where the time goes in v4:
time: 20.8 us; the launch traced here: 20.7 us
  Pallas kernels  20 us (96%)
  local copies, waits for them, and re-layouts  0.61 us (3%)
    pallas_call x1, Pallas kernels, per_device(): pl.pallas_call(functools.partial(kernel, groups), out_shape=pltpu.VMEM((5...  20 us
    unnamed x1, local copies, waits for them, and re-layouts  0.61 us

profile of v4, /device:TPU:8, one launch (start us, length us, event | category | flops | bytes accessed | tf_op | source)
XLA Modules:
  0.0 20.7 jit_solution(2739975528668024474)
XLA Ops:
  0.0 20.0 %shard_map.82 = f32[5,768]{1,0:T(8,128)S(1)} custom-call(f32[5,768]{1,0:T(8,128)} %state_h.1, bf16[20,40,768]{2,1,0:T(8,128)(2,1)} %pinv_h.1, s32[40,768]{1,0:T(8,128)} %sten_h.1, s32[32,64]{1,0:T(8,128)} %send_h.1, s32[2,128]{1,0:T(2,128)} %gids_h.1, s32[2,1536]{1,0:T(2,128)} %fc_h.1, f32[4,1536]{1,0:T(4,128)} %fg_h.1, bf16[80,1536]{1,0:T(8,128)(2,1)} %fb_h.1), custom_call_target="tpu_custom_call" | custom-call | tf_op jit(solution)/shard_map/pallas_call | solution.py:598
  20.1 0.6 %copy.10 = f32[5,768]{1,0:T(8,128)} copy(f32[5,768]{1,0:T(8,128)S(1)} %shard_map.82) | data formatting | bytes 30720

commit v5 on v3

--- a/solution.py
+++ b/solution.py
@@ -534,9 +534,12 @@
                 rows = [jnp.where(mask, high, 0.0), jnp.where(mask, rest, 0.0)]
                 place = (e * CT + t) * 16
                 wl[place : place + 16, at] = jnp.concatenate(rows, axis=0).astype(BF16)
-    total = lax.dot_general(
-        wl[...], hot[...], (((1,), (1,)), ((), ())), preferred_element_type=F32
-    )
+        if ft % 4 == 3:
+            at = slice((ft - 3) * 128, (ft + 1) * 128)
+            summed = lax.dot_general(
+                wl[:, at], hot[:, at], (((1,), (1,)), ((), ())), preferred_element_type=F32
+            )
+            total = summed if ft == 3 else total + summed
     for t in range(CT):
         gained = total[t * 16 : t * 16 + 16, 0:128]
         lost = total[(CT + t) * 16 : (CT + t) * 16 + 16, 128:256]

time: 21 us -> 21 us (level)
  no operation moved by 1% of the time
where the time goes in v5:
time: 21 us; the launch traced here: 20.9 us
  Pallas kernels  20.2 us (96%)
  local copies, waits for them, and re-layouts  0.61 us (3%)
    pallas_call x1, Pallas kernels, per_device(): pl.pallas_call(functools.partial(kernel, groups), out_shape=pltpu.VMEM((5...  20.2 us
    unnamed x1, local copies, waits for them, and re-layouts  0.61 us

profile of v5, /device:TPU:8, one launch (start us, length us, event | category | flops | bytes accessed | tf_op | source)
XLA Modules:
  0.0 20.9 jit_solution(10391144274169968589)
XLA Ops:
  0.0 20.2 %shard_map.82 = f32[5,768]{1,0:T(8,128)S(1)} custom-call(f32[5,768]{1,0:T(8,128)} %state_h.1, bf16[20,40,768]{2,1,0:T(8,128)(2,1)} %pinv_h.1, s32[40,768]{1,0:T(8,128)} %sten_h.1, s32[32,64]{1,0:T(8,128)} %send_h.1, s32[2,128]{1,0:T(2,128)} %gids_h.1, s32[2,1536]{1,0:T(2,128)} %fc_h.1, f32[4,1536]{1,0:T(4,128)} %fg_h.1, bf16[80,1536]{1,0:T(8,128)(2,1)} %fb_h.1), custom_call_target="tpu_custom_call" | custom-call | tf_op jit(solution)/shard_map/pallas_call | solution.py:596
  20.3 0.6 %copy.10 = f32[5,768]{1,0:T(8,128)} copy(f32[5,768]{1,0:T(8,128)S(1)} %shard_map.82) | data formatting | bytes 30720
